TPU v7x, 128 devices: a whole 4x4x4 slice. The times are simulated.
128 devices in a mesh: slab: 4 (over y), tile: 32 (over z, x, core).
Axes of the slice: x: 4, y: 4, z: 4, core: 2. Of those that a mesh axis runs over, the one named last changes fastest.
Arguments:
- coarse: bfloat16 [1048576, 256], P(('slab', 'tile')), may hold values from -6 to 6
- counts: int32 [128], P(('slab', 'tile')), may hold values from 1 to 1024, 65536 in all
- subdivided: int32 [128, 1024], P(('slab', 'tile')), may hold values from 0 to 8191, as said below
- requested: int32 [128, 128, 8], P(('slab', 'tile')), may hold values from -1 to 511, as said below
- neighbours: int32 [26, 65536], P(None, ('slab', 'tile')), may hold values from 0 to 1536
- up_weight: bfloat16 [256, 1024], replicated, may hold values from -0.375 to 0.375
- first_conv: bfloat16 [3456, 128], replicated, may hold values from -0.109375 to 0.109375
- second_conv: bfloat16 [3456, 128], replicated, may hold values from -0.109375 to 0.109375
- occupancy_weight: bfloat16 [128], replicated, may hold values from -0.5 to 0.5
Outputs:
- features: bfloat16 [65536, 1024], P(('slab', 'tile'))
- occupancy: float32 [8, 65536], P(None, ('slab', 'tile'))
Inputs may be any that keep to these rules, and one draw needn't show every extreme that they name: The counts sum to 65536. `subdivided`: row h holds distinct cells of home device h; only its first counts[h] entries are read. requested[d, p, :] holds distinct slots of device p, then -1 for unused entries; every device reads 8 blocks from some other device; requested[d, d, :] is all -1.
All inputs are finite; a program needn't handle non-finite values.
Results may differ from a plain program's by a relative error of at most 0.0054.
Values may be sent and summed in bfloat16 or wider, within the bound.
No kernel may reach another device: no remote copies, remote signals or barrier semaphores. Data moves between devices by JAX's collectives and lax.ppermute only.
A program may use at most 128 MiB of HBM per device.

v0:
```python
import functools

import jax
import jax.numpy as jnp
import numpy as np
from jax import lax
from jax.experimental import pallas as pl
from jax.experimental.pallas import tpu as pltpu
from jax.sharding import PartitionSpec as P

AXES = ("slab", "tile")
F32 = jnp.float32
BF16 = jnp.bfloat16
VMEM_LIMIT = 58 * 2**20
VM = pl.BlockSpec(memory_space=pltpu.VMEM)
SM = pl.BlockSpec(memory_space=pltpu.SMEM)
UNROLL = 64


def axis_children(offset):
    if offset == -1:
        return ([1], [0])
    if offset == 1:
        return ([0], [1])
    return ([0, 1], [0, 1])


def neighbour_plan():
    plans = []
    for near in np.ndindex(3, 3, 3):
        near = [v - 1 for v in near]
        parts = [axis_children(v) for v in near]
        sources = [(a, b, c) for a in parts[0][0] for b in parts[1][0] for c in parts[2][0]]
        targets = [(a, b, c) for a in parts[0][1] for b in parts[1][1] for c in parts[2][1]]
        taps = []
        for s in sources:
            row = []
            for t in targets:
                o = [2 * near[i] + s[i] - t[i] for i in range(3)]
                row.append(9 * (o[0] + 1) + 3 * (o[1] + 1) + o[2] + 1)
            taps.append(row)
        code = lambda v: 4 * v[0] + 2 * v[1] + v[2]
        plans.append(([code(s) for s in sources], [code(t) for t in targets], taps))
    return plans


PLANS = neighbour_plan()


def tap_block(w_ref, tap):
    return w_ref[tap * 128 : (tap + 1) * 128, :]


def tap_matrix(w_ref, taps):
    return jnp.concatenate(
        [jnp.concatenate([tap_block(w_ref, t) for t in row], axis=1) for row in taps], axis=0
    )


def dot(a, b):
    return jnp.dot(a, b, preferred_element_type=F32)


def convolve(idx_ref, own_ref, w_ref, table, picked, total):
    blocks = own_ref.shape[0]
    sources, targets, taps = PLANS[13]
    for pair in range(4):
        cols = tap_matrix(w_ref, [row[2 * pair : 2 * pair + 2] for row in taps])
        part = dot(own_ref[...], cols)
        total[2 * pair] = part[:, :128]
        total[2 * pair + 1] = part[:, 128:]
    for t in range(26):
        sources, targets, taps = PLANS[t if t < 13 else t + 1]

        def some_rows(i, carry, t=t):
            base = t * blocks + i * UNROLL
            at = pl.multiple_of(i * (UNROLL * 8), UNROLL * 8)
            rows = [
                table[pl.ds(pl.multiple_of(idx_ref[base + u], 8), 8), :] for u in range(UNROLL)
            ]
            for u in range(UNROLL):
                picked[pl.ds(at + u * 8, 8), :] = rows[u]
            return carry

        lax.fori_loop(0, blocks // UNROLL, some_rows, 0)
        left = jnp.concatenate(
            [picked[pl.ds(s, blocks, stride=8), :].astype(BF16) for s in sources], axis=1
        )
        step = min(2, len(targets))
        for j in range(0, len(targets), step):
            part = dot(left, tap_matrix(w_ref, [row[j : j + step] for row in taps]))
            for k in range(step):
                total[targets[j + k]] += part[:, k * 128 : (k + 1) * 128]


def silu(x):
    return x * jax.nn.sigmoid(x)


def roll_kernel(me_ref, got_ref, home_ref, out_ref):
    devices = got_ref.shape[0]
    me = me_ref[0]
    ids = lax.broadcasted_iota(jnp.int32, (devices, 1), 0)
    lower = jnp.sum(jnp.where(ids < me, got_ref[:, 8:9], 0))
    shift = lax.rem(lower, devices)

    def one(d, carry):
        src = lax.rem(d - shift + devices, devices)
        out_ref[d] = home_ref[src]
        return carry

    lax.fori_loop(0, devices, one, 0, unroll=8)


def select_rows(got_ref, source, scratch, out_ref):
    devices = got_ref.shape[0]
    blocks, width = source.shape
    lanes = lax.broadcasted_iota(jnp.int32, (devices, blocks), 1)
    for k in range(8):
        pick = (got_ref[:, k : k + 1] == lanes).astype(BF16)
        part = dot(pick, source)
        for c in range(width // 128):
            scratch[c, pl.ds(k, devices, stride=8), :] = part[:, c * 128 : (c + 1) * 128]
    for c in range(width // 128):
        out_ref[:, :, c * 128 : (c + 1) * 128] = (
            scratch[c].astype(BF16).reshape(devices, 8, 128)
        )


def parent_kernel(me_ref, got_ref, arrived_ref, parent_ref, send_ref, scratch):
    devices = got_ref.shape[0]
    blocks = parent_ref.shape[0]
    me = me_ref[0]
    cols = devices * 8
    home = lax.broadcasted_iota(jnp.int32, (devices, cols), 1) // 8
    row = lax.broadcasted_iota(jnp.int32, (devices, cols), 0)
    counts = got_ref[:, 8:9]
    lower = jnp.sum(jnp.where(row < home, counts, 0), axis=0, keepdims=True)
    upper = jnp.sum(jnp.where(row <= home, counts, 0), axis=0, keepdims=True)
    within = lax.broadcasted_iota(jnp.int32, (1, cols), 1) % 8
    slot = (lower - me + devices - 1) // devices + within
    slot = jnp.where(slot * devices + me < upper, slot, -1)
    pick = (lax.broadcasted_iota(jnp.int32, (blocks, cols), 0) == slot).astype(BF16)
    parent = dot(pick, arrived_ref[...]).astype(BF16)
    parent_ref[...] = parent
    select_rows(got_ref, parent, scratch, send_ref)


def first_kernel(
    idx_ref, got_ref, parent_ref, far_ref, up_ref, w_ref,
    child_ref, hidden_ref, send_ref, table, picked, total, scratch,
):
    blocks = parent_ref.shape[0]
    rows = 128

    def lift(parents, base):
        made = silu(dot(parents, up_ref[...])).astype(BF16)
        for q in range(8):
            table[pl.ds(base * 8 + q, rows, stride=8), :] = (
                made[:, q * 128 : (q + 1) * 128].astype(F32)
            )
        return made

    def own_rows(i, carry):
        at = pl.ds(pl.multiple_of(i * rows, rows), rows)
        child_ref[at, :] = lift(parent_ref[at, :], pl.multiple_of(i * rows, rows))
        return carry

    def far_rows(i, carry):
        at = pl.ds(pl.multiple_of(i * rows, rows), rows)
        lift(far_ref[at, :], pl.multiple_of(blocks + i * rows, rows))
        return carry

    lax.fori_loop(0, blocks // rows, own_rows, 0)
    lax.fori_loop(0, far_ref.shape[0] // rows, far_rows, 0)
    last = (blocks + far_ref.shape[0]) * 8
    table[last : last + 8, :] = jnp.zeros((8, 128), F32)
    convolve(idx_ref, child_ref, w_ref, table, picked, total)
    for q in range(8):
        hidden_ref[:, q * 128 : (q + 1) * 128] = silu(total[q]).astype(BF16)
    select_rows(got_ref, hidden_ref[...], scratch, send_ref)


def second_kernel(
    idx_ref, child_ref, hidden_ref, far_ref, w_ref, occ_ref,
    feature_ref, occupancy_ref, table, picked, total,
):
    blocks = hidden_ref.shape[0]
    rows = 128

    def fill(ref, base):
        def some(i, carry):
            at = pl.ds(pl.multiple_of(i * rows, rows), rows)
            to = pl.multiple_of((base + i * rows) * 8, rows * 8)
            for q in range(8):
                table[pl.ds(to + q, rows, stride=8), :] = (
                    ref[at, q * 128 : (q + 1) * 128].astype(F32)
                )
            return carry

        lax.fori_loop(0, ref.shape[0] // rows, some, 0)

    fill(hidden_ref, 0)
    far = far_ref.shape[0]
    fill(far_ref, blocks)
    last = (blocks + far) * 8
    table[last : last + 8, :] = jnp.zeros((8, 128), F32)
    convolve(idx_ref, hidden_ref, w_ref, table, picked, total)
    for q in range(8):
        at = slice(q * 128, (q + 1) * 128)
        feature_ref[:, at] = (child_ref[:, at].astype(F32) + total[q]).astype(BF16)
    lane = lax.broadcasted_iota(jnp.int32, (8, 1024), 1) // 128
    row = lax.broadcasted_iota(jnp.int32, (8, 1024), 0)
    head = jnp.where(lane == row, jnp.concatenate([occ_ref[...].astype(F32)] * 8, axis=1), 0.0)
    occupancy_ref[...] = lax.dot_general(
        head.astype(BF16), feature_ref[...], (((1,), (1,)), ((), ())), preferred_element_type=F32
    )


def shape(*dims, dtype=BF16):
    return jax.ShapeDtypeStruct(dims, dtype)


def call(kernel, out_shape, in_specs, scratch=()):
    return pl.pallas_call(
        kernel,
        out_shape=out_shape,
        in_specs=in_specs,
        out_specs=jax.tree.map(lambda _: VM, out_shape),
        scratch_shapes=list(scratch),
        compiler_params=pltpu.CompilerParams(vmem_limit_bytes=VMEM_LIMIT),
    )


def exchange(x):
    return lax.all_to_all(x, AXES, split_axis=0, concat_axis=0, tiled=True)


def body(
    coarse, counts, subdivided, requested, neighbours,
    up_weight, first_conv, second_conv, occupancy_weight,
):
    devices = lax.axis_size(AXES)
    me = lax.axis_index(AXES).astype(jnp.int32).reshape(1)
    blocks = neighbours.shape[1]
    far = devices * 8
    table_rows = (blocks + far + 8) * 8

    note = jnp.concatenate(
        [requested[0], jnp.broadcast_to(counts[:, None], (devices, 8))], axis=1
    )
    got = exchange(note.reshape(devices, 1, 16)).reshape(devices, 16)
    order = subdivided[0].reshape(8, devices).T.reshape(-1)
    home = coarse[order].reshape(devices, 8, -1)
    idx = (neighbours * 8).reshape(-1)

    leaving = call(roll_kernel, shape(devices, 8, 256), [SM, VM, VM])(me, got, home)
    arrived = exchange(leaving)
    parent, send = call(
        parent_kernel,
        (shape(blocks, 256), shape(devices, 8, 256)),
        [SM, VM, VM],
        [pltpu.VMEM((2, far, 128), F32)],
    )(me, got, arrived.reshape(far, 256))
    far_parent = exchange(send).reshape(far, 256)

    work = [
        pltpu.VMEM((table_rows, 128), F32),
        pltpu.VMEM((blocks * 8, 128), F32),
        pltpu.VMEM((8, blocks, 128), F32),
    ]
    child, hidden, send = call(
        first_kernel,
        (shape(blocks, 1024), shape(blocks, 1024), shape(devices, 8, 1024)),
        [SM] + [VM] * 5,
        work + [pltpu.VMEM((8, far, 128), F32)],
    )(idx, got, parent, far_parent, up_weight, first_conv)
    far_hidden = exchange(send).reshape(far, 1024)
    return tuple(
        call(
            second_kernel,
            (shape(blocks, 1024), shape(8, blocks, dtype=F32)),
            [SM] + [VM] * 5,
            work,
        )(idx, child, hidden, far_hidden, second_conv, occupancy_weight.reshape(1, 128))
    )


def solution(mesh):
    rows = P(AXES, None)
    in_specs = (rows, P(AXES), rows, P(AXES, None, None), P(None, AXES), P(), P(), P(), P())
    out_specs = (rows, P(None, AXES))
    return jax.shard_map(body, mesh=mesh, in_specs=in_specs, out_specs=out_specs, check_vma=False)
```

profile of v0, /device:TPU:1, one launch (start us, length us, event | category | flops | bytes accessed | tf_op | source)
XLA Modules:
  0.0 161.9 jit_solution(5443925081726589189)
XLA Ops:
  1.3 0.8 copy.14
  2.1 0.6 concatenate.3
  2.7 11.5 %all-to-all-start = ((s32[128,1,16]{2,1,0:T(1,128)}), s32[128,1,16]{2,1,0:T(1,128)S(1)}, u32[]{:S(2)}, u32[]{:S(2)}) async-start(s32[128,1,16]{2,1,0:T(1,128)} %bitcast.2), calls=%async_computation | async-start | bytes 131072 | tf_op jit(solution)/shard_map/all_to_all | solution.py:236
  14.2 0.8 copy.15
  15.0 0.1 reshape.67
  15.1 0.0 copy-start.2
  15.1 7.4 %gather_fusion = bf16[1024,256]{1,0:T(8,128)(2,1)} fusion(bf16[8192,256]{1,0:T(8,128)(2,1)} %param.9, s32[1024]{0:T(1024)S(1)} %broadcast_clamp_fusion), kind=kCustom, calls=%fused_computation | custom fusion | bytes 1052672 | tf_op jit(solution)/shard_map/gather | solution.py:254
  22.5 1.2 all-to-all-done
  23.7 0.0 copy-start.1
  23.7 0.6 copy-done.1
  24.3 2.5 %shard_map.104 = bf16[128,8,256]{2,1,0:T(8,128)(2,1)} custom-call(s32[1]{0:T(128)} %bitcast.4.me_ref, s32[128,16]{1,0:T(8,128)} %bitcast.18, bf16[128,8,256]{2,1,0:T(8,128)(2,1)} %bitcast.17), custom_call_target="tpu_custom_call" | custom-call | tf_op jit(solution)/shard_map/pallas_call | solution.py:257
  26.8 22.4 %all_to_all.20 = bf16[128,8,256]{2,1,0:T(8,128)(2,1)} all-to-all(bf16[128,8,256]{2,1,0:T(8,128)(2,1)} %shard_map.104), channel_id=1, replica_groups=mesh['slab'=4,'tile'=32] {'slab','tile'}, dimensions={0} | all-to-all | bytes 1048576 | tf_op jit(solution)/shard_map/all_to_all | solution.py:236
  49.2 3.4 %shard_map.105 = (bf16[512,256]{1,0:T(8,128)(2,1)}, bf16[128,8,256]{2,1,0:T(8,128)(2,1)}) custom-call(s32[1]{0:T(128)} %bitcast.4.me_ref, s32[128,16]{1,0:T(8,128)} %bitcast.19, bf16[1024,256]{1,0:T(8,128)(2,1)} %bitcast.15), custom_call_target="tpu_custom_call" | custom-call | tf_op jit(solution)/shard_map/pallas_call | solution.py:259
  52.6 4.5 %all-to-all-start.2 = ((bf16[128,8,256]{2,1,0:T(8,128)(2,1)}), bf16[128,8,256]{2,1,0:T(8,128)(2,1)S(1)}, u32[]{:S(2)}, u32[]{:S(2)}) async-start(bf16[128,8,256]{2,1,0:T(8,128)(2,1)} %get-tuple-element.8), calls=%async_computation.2 | async-start | bytes 1048576 | tf_op jit(solution)/shard_map/all_to_all | solution.py:236
  57.1 0.0 copy-done.2
  57.1 0.6 reshape.63.idx_ref
  57.8 13.1 %all-to-all-done.2 = bf16[128,8,256]{2,1,0:T(8,128)(2,1)S(1)} async-done(((bf16[128,8,256]{2,1,0:T(8,128)(2,1)}), bf16[128,8,256]{2,1,0:T(8,128)(2,1)S(1)}, u32[]{:S(2)}, u32[]{:S(2)}) %all-to-all-start.2) | async-done | bytes 524320 | tf_op jit(solution)/shard_map/all_to_all | solution.py:236
  70.8 0.0 copy-start
  70.8 0.8 copy-done
  71.6 28.8 %shard_map.106 = (bf16[512,1024]{1,0:T(8,128)(2,1)}, bf16[512,1024]{1,0:T(8,128)(2,1)}, bf16[128,8,1024]{2,1,0:T(8,128)(2,1)}) custom-call(s32[13312]{0:T(1024)} %reshape.63.idx_ref, s32[128,16]{1,0:T(8,128)} %bitcast.20, bf16[512,256]{1,0:T(8,128)(2,1)} %get-tuple-element.7.parent_ref, bf16[1024,256]{1,0:T(8,128)(2,1)} %bitcast.16, ...), custom_call_target="tpu_custom_call" | custom-call | tf_op jit(solution)/shard_map/pallas_call | solution.py:272
  100.4 35.9 %all_to_all.21 = bf16[128,8,1024]{2,1,0:T(8,128)(2,1)} all-to-all(bf16[128,8,1024]{2,1,0:T(8,128)(2,1)} %get-tuple-element.11), channel_id=1, replica_groups=mesh['slab'=4,'tile'=32] {'slab','tile'}, dimensions={0} | all-to-all | bytes 4194304 | tf_op jit(solution)/shard_map/all_to_all | solution.py:236
  136.3 25.6 %shard_map.107 = (bf16[512,1024]{1,0:T(8,128)(2,1)}, f32[8,512]{1,0:T(8,128)}) custom-call(s32[13312]{0:T(1024)} %reshape.63.idx_ref, bf16[512,1024]{1,0:T(8,128)(2,1)} %get-tuple-element.9.child_ref, bf16[512,1024]{1,0:T(8,128)(2,1)} %get-tuple-element.10.hidden_ref, bf16[1024,1024]{1,0:T(8,128)(2,1)} %bitcast.14, bf16[3456,128]{1,0:T(8,128)(2,1)} %w_ref.3, ...), custom_call_target="tpu_custom_call" | custom-call | tf_op jit(solution)/shard_map/pallas_call | solution.py:280
  (3 shorter events, 0.0 us)
Async XLA Ops:
  2.7 21.0 %all-to-all-start = ((s32[128,1,16]{2,1,0:T(1,128)}), s32[128,1,16]{2,1,0:T(1,128)S(1)}, u32[]{:S(2)}, u32[]{:S(2)}) async-start(s32[128,1,16]{2,1,0:T(1,128)} %bitcast.2), calls=%async_computation | async-start | bytes 131072 | tf_op jit(solution)/shard_map/all_to_all | solution.py:236
  15.1 42.0 %copy-start.2 = (s32[26,512]{1,0:T(8,128)S(1)}, s32[26,512]{1,0:T(8,128)}, u32[]{:S(2)}) copy-start(s32[26,512]{1,0:T(8,128)} %param.13) | copy-start | bytes 159748
  23.7 0.6 copy-start.1
  52.6 18.2 %all-to-all-start.2 = ((bf16[128,8,256]{2,1,0:T(8,128)(2,1)}), bf16[128,8,256]{2,1,0:T(8,128)(2,1)S(1)}, u32[]{:S(2)}, u32[]{:S(2)}) async-start(bf16[128,8,256]{2,1,0:T(8,128)(2,1)} %get-tuple-element.8), calls=%async_computation.2 | async-start | bytes 1048576 | tf_op jit(solution)/shard_map/all_to_all | solution.py:236
  70.8 0.8 copy-start
where the time goes:
time: 162 us
  Pallas kernels  60.2 us (37%)
  blocking collectives  58.3 us (36%)
  starting transfers between devices  16 us (10%)
  waiting for transfers between devices  14.3 us (9%)
  local copies, waits for them, and re-layouts  11.7 us (7%)
    all_to_all x2, blocking collectives, exchange(): return lax.all_to_all(x, AXES, split_axis=0, concat_axis=0, tiled=True)  58.3 us
    pallas_call x1, Pallas kernels, body(): call(first_kernel, (shape(blocks, 1024), shape(blocks, 1024), shape(devic...  28.8 us
    pallas_call x1, Pallas kernels, body(): call(second_kernel, (shape(blocks, 1024), shape(8, blocks, dtype=F32)), [...  25.6 us
    all_to_all x2, starting transfers between devices, exchange(): return lax.all_to_all(x, AXES, split_axis=0, concat_axis=0, tiled=True)  16 us
    all_to_all x2, waiting for transfers between devices, exchange(): return lax.all_to_all(x, AXES, split_axis=0, concat_axis=0, tiled=True)  14.3 us
    gather x1, local copies, waits for them, and re-layouts, body(): home = coarse[order].reshape(devices, 8, -1)  7.37 us
    pallas_call x1, Pallas kernels, body(): call(parent_kernel, (shape(blocks, 256), shape(devices, 8, 256)), [SM, VM...  3.35 us
  transfers between devices with their start and end apart: 2, of which 2 were waited for; matrix products, arithmetic and copies ran while one was open for 6% of the time, Pallas kernels for 0%

commit v1 on v0

--- a/solution.py
+++ b/solution.py
@@ -14,7 +14,7 @@
 VMEM_LIMIT = 58 * 2**20
 VM = pl.BlockSpec(memory_space=pltpu.VMEM)
 SM = pl.BlockSpec(memory_space=pltpu.SMEM)
-UNROLL = 64
+GROUP = 32
 
 
 def axis_children(offset):
@@ -63,34 +63,44 @@
 
 def convolve(idx_ref, own_ref, w_ref, table, picked, total):
     blocks = own_ref.shape[0]
-    sources, targets, taps = PLANS[13]
-    for pair in range(4):
-        cols = tap_matrix(w_ref, [row[2 * pair : 2 * pair + 2] for row in taps])
-        part = dot(own_ref[...], cols)
-        total[2 * pair] = part[:, :128]
-        total[2 * pair + 1] = part[:, 128:]
-    for t in range(26):
-        sources, targets, taps = PLANS[t if t < 13 else t + 1]
-
-        def some_rows(i, carry, t=t):
-            base = t * blocks + i * UNROLL
-            at = pl.multiple_of(i * (UNROLL * 8), UNROLL * 8)
+
+    def pick(t):
+        into = picked[t % 2]
+        for first in range(t * blocks, (t + 1) * blocks, GROUP):
             rows = [
-                table[pl.ds(pl.multiple_of(idx_ref[base + u], 8), 8), :] for u in range(UNROLL)
+                table[pl.ds(pl.multiple_of(idx_ref[first + u], 8), 8), :] for u in range(GROUP)
             ]
-            for u in range(UNROLL):
-                picked[pl.ds(at + u * 8, 8), :] = rows[u]
-            return carry
-
-        lax.fori_loop(0, blocks // UNROLL, some_rows, 0)
-        left = jnp.concatenate(
-            [picked[pl.ds(s, blocks, stride=8), :].astype(BF16) for s in sources], axis=1
-        )
+            at = (first - t * blocks) * 8
+            for u in range(GROUP):
+                into[at + u * 8 : at + u * 8 + 8, :] = rows[u]
+
+    def add(left, plan, fresh):
+        sources, targets, taps = plan
         step = min(2, len(targets))
         for j in range(0, len(targets), step):
             part = dot(left, tap_matrix(w_ref, [row[j : j + step] for row in taps]))
             for k in range(step):
-                total[targets[j + k]] += part[:, k * 128 : (k + 1) * 128]
+                piece = part[:, k * 128 : (k + 1) * 128]
+                if fresh:
+                    total[targets[j + k]] = piece
+                else:
+                    total[targets[j + k]] += piece
+
+    for t in range(-1, 26):
+
+        def step(i, carry, t=t):
+            if t + 1 < 26:
+                pick(t + 1)
+            if t < 0:
+                add(own_ref[...], PLANS[13], True)
+            else:
+                plan = PLANS[t if t < 13 else t + 1]
+                near = picked[t % 2]
+                left = [near[pl.ds(s, blocks, stride=8), :].astype(BF16) for s in plan[0]]
+                add(jnp.concatenate(left, axis=1), plan, False)
+            return carry
+
+        lax.fori_loop(0, 1, step, 0)
 
 
 def silu(x):
@@ -266,7 +276,7 @@
 
     work = [
         pltpu.VMEM((table_rows, 128), F32),
-        pltpu.VMEM((blocks * 8, 128), F32),
+        (pltpu.VMEM((blocks * 8, 128), F32),) * 2,
         pltpu.VMEM((8, blocks, 128), F32),
     ]
     child, hidden, send = call(

time: 162 us -> 148 us (0.914)
  Pallas kernels: 60.2 us -> 45.4 us
    pallas_call x1, Pallas kernels: 28.8 us -> 21.2 us  [body(): call(first_kernel, (shape(blocks, 1024), shape(blocks, 1024), shape(devic...]
    pallas_call x1, Pallas kernels: 25.6 us -> 18.3 us  [body(): call(second_kernel, (shape(blocks, 1024), shape(8, blocks, dtype=F32)), [...]
where the time goes in v1:
time: 148 us; the launch traced here: 147 us
  blocking collectives  58.3 us (39%)
  Pallas kernels  45.4 us (31%)
  starting transfers between devices  16 us (11%)
  waiting for transfers between devices  14.3 us (10%)
  local copies, waits for them, and re-layouts  11.7 us (8%)
    all_to_all x2, blocking collectives, exchange(): return lax.all_to_all(x, AXES, split_axis=0, concat_axis=0, tiled=True)  58.3 us
    pallas_call x1, Pallas kernels, body(): call(first_kernel, (shape(blocks, 1024), shape(blocks, 1024), shape(devic...  21.2 us
    pallas_call x1, Pallas kernels, body(): call(second_kernel, (shape(blocks, 1024), shape(8, blocks, dtype=F32)), [...  18.3 us
    all_to_all x2, starting transfers between devices, exchange(): return lax.all_to_all(x, AXES, split_axis=0, concat_axis=0, tiled=True)  16 us
    all_to_all x2, waiting for transfers between devices, exchange(): return lax.all_to_all(x, AXES, split_axis=0, concat_axis=0, tiled=True)  14.3 us
    gather x1, local copies, waits for them, and re-layouts, body(): home = coarse[order].reshape(devices, 8, -1)  7.37 us
    pallas_call x1, Pallas kernels, body(): call(parent_kernel, (shape(blocks, 256), shape(devices, 8, 256)), [SM, VM...  3.35 us
  transfers between devices with their start and end apart: 2, of which 2 were waited for; matrix products, arithmetic and copies ran while one was open for 6% of the time, Pallas kernels for 0%

profile of v1, /device:TPU:1, one launch (start us, length us, event | category | flops | bytes accessed | tf_op | source)
XLA Modules:
  0.0 147.1 jit_solution(6709729801907009193)
XLA Ops:
  1.3 0.8 copy.14
  2.1 0.6 concatenate.3
  2.7 11.5 %all-to-all-start = ((s32[128,1,16]{2,1,0:T(1,128)}), s32[128,1,16]{2,1,0:T(1,128)S(1)}, u32[]{:S(2)}, u32[]{:S(2)}) async-start(s32[128,1,16]{2,1,0:T(1,128)} %bitcast.2), calls=%async_computation | async-start | bytes 131072 | tf_op jit(solution)/shard_map/all_to_all | solution.py:246
  14.2 0.8 copy.15
  15.0 0.1 reshape.67
  15.1 0.0 copy-start.2
  15.1 7.4 %gather_fusion = bf16[1024,256]{1,0:T(8,128)(2,1)} fusion(bf16[8192,256]{1,0:T(8,128)(2,1)} %param.9, s32[1024]{0:T(1024)S(1)} %broadcast_clamp_fusion), kind=kCustom, calls=%fused_computation | custom fusion | bytes 1052672 | tf_op jit(solution)/shard_map/gather | solution.py:264
  22.5 1.2 all-to-all-done
  23.7 0.0 copy-start.1
  23.7 0.6 copy-done.1
  24.3 2.5 %shard_map.104 = bf16[128,8,256]{2,1,0:T(8,128)(2,1)} custom-call(s32[1]{0:T(128)} %bitcast.4.me_ref, s32[128,16]{1,0:T(8,128)} %bitcast.18, bf16[128,8,256]{2,1,0:T(8,128)(2,1)} %bitcast.17), custom_call_target="tpu_custom_call" | custom-call | tf_op jit(solution)/shard_map/pallas_call | solution.py:267
  26.8 22.4 %all_to_all.20 = bf16[128,8,256]{2,1,0:T(8,128)(2,1)} all-to-all(bf16[128,8,256]{2,1,0:T(8,128)(2,1)} %shard_map.104), channel_id=1, replica_groups=mesh['slab'=4,'tile'=32] {'slab','tile'}, dimensions={0} | all-to-all | bytes 1048576 | tf_op jit(solution)/shard_map/all_to_all | solution.py:246
  49.2 3.4 %shard_map.105 = (bf16[512,256]{1,0:T(8,128)(2,1)}, bf16[128,8,256]{2,1,0:T(8,128)(2,1)}) custom-call(s32[1]{0:T(128)} %bitcast.4.me_ref, s32[128,16]{1,0:T(8,128)} %bitcast.19, bf16[1024,256]{1,0:T(8,128)(2,1)} %bitcast.15), custom_call_target="tpu_custom_call" | custom-call | tf_op jit(solution)/shard_map/pallas_call | solution.py:269
  52.6 4.5 %all-to-all-start.2 = ((bf16[128,8,256]{2,1,0:T(8,128)(2,1)}), bf16[128,8,256]{2,1,0:T(8,128)(2,1)S(1)}, u32[]{:S(2)}, u32[]{:S(2)}) async-start(bf16[128,8,256]{2,1,0:T(8,128)(2,1)} %get-tuple-element.8), calls=%async_computation.2 | async-start | bytes 1048576 | tf_op jit(solution)/shard_map/all_to_all | solution.py:246
  57.1 0.0 copy-done.2
  57.1 0.6 reshape.63.idx_ref
  57.7 13.1 %all-to-all-done.2 = bf16[128,8,256]{2,1,0:T(8,128)(2,1)S(1)} async-done(((bf16[128,8,256]{2,1,0:T(8,128)(2,1)}), bf16[128,8,256]{2,1,0:T(8,128)(2,1)S(1)}, u32[]{:S(2)}, u32[]{:S(2)}) %all-to-all-start.2) | async-done | bytes 524320 | tf_op jit(solution)/shard_map/all_to_all | solution.py:246
  70.8 0.0 copy-start
  70.8 0.8 copy-done
  71.6 21.2 %shard_map.106 = (bf16[512,1024]{1,0:T(8,128)(2,1)}, bf16[512,1024]{1,0:T(8,128)(2,1)}, bf16[128,8,1024]{2,1,0:T(8,128)(2,1)}) custom-call(s32[13312]{0:T(1024)} %reshape.63.idx_ref, s32[128,16]{1,0:T(8,128)} %bitcast.20, bf16[512,256]{1,0:T(8,128)(2,1)} %get-tuple-element.7.parent_ref, bf16[1024,256]{1,0:T(8,128)(2,1)} %bitcast.16, ...), custom_call_target="tpu_custom_call" | custom-call | tf_op jit(solution)/shard_map/pallas_call | solution.py:282
  92.9 35.9 %all_to_all.21 = bf16[128,8,1024]{2,1,0:T(8,128)(2,1)} all-to-all(bf16[128,8,1024]{2,1,0:T(8,128)(2,1)} %get-tuple-element.11), channel_id=1, replica_groups=mesh['slab'=4,'tile'=32] {'slab','tile'}, dimensions={0} | all-to-all | bytes 4194304 | tf_op jit(solution)/shard_map/all_to_all | solution.py:246
  128.8 18.3 %shard_map.107 = (bf16[512,1024]{1,0:T(8,128)(2,1)}, f32[8,512]{1,0:T(8,128)}) custom-call(s32[13312]{0:T(1024)} %reshape.63.idx_ref, bf16[512,1024]{1,0:T(8,128)(2,1)} %get-tuple-element.9.child_ref, bf16[512,1024]{1,0:T(8,128)(2,1)} %get-tuple-element.10.hidden_ref, bf16[1024,1024]{1,0:T(8,128)(2,1)} %bitcast.14, bf16[3456,128]{1,0:T(8,128)(2,1)} %w_ref.3, ...), custom_call_target="tpu_custom_call" | custom-call | tf_op jit(solution)/shard_map/pallas_call | solution.py:290
  (3 shorter events, 0.0 us)
Async XLA Ops:
  2.7 21.0 %all-to-all-start = ((s32[128,1,16]{2,1,0:T(1,128)}), s32[128,1,16]{2,1,0:T(1,128)S(1)}, u32[]{:S(2)}, u32[]{:S(2)}) async-start(s32[128,1,16]{2,1,0:T(1,128)} %bitcast.2), calls=%async_computation | async-start | bytes 131072 | tf_op jit(solution)/shard_map/all_to_all | solution.py:246
  15.1 42.0 %copy-start.2 = (s32[26,512]{1,0:T(8,128)S(1)}, s32[26,512]{1,0:T(8,128)}, u32[]{:S(2)}) copy-start(s32[26,512]{1,0:T(8,128)} %param.13) | copy-start | bytes 159748
  23.7 0.6 copy-start.1
  52.6 18.2 %all-to-all-start.2 = ((bf16[128,8,256]{2,1,0:T(8,128)(2,1)}), bf16[128,8,256]{2,1,0:T(8,128)(2,1)S(1)}, u32[]{:S(2)}, u32[]{:S(2)}) async-start(bf16[128,8,256]{2,1,0:T(8,128)(2,1)} %get-tuple-element.8), calls=%async_computation.2 | async-start | bytes 1048576 | tf_op jit(solution)/shard_map/all_to_all | solution.py:246
  70.8 0.8 copy-start

commit v2 on v1

v2 whole, which is shorter than its diff:
```python
import functools

import jax
import jax.numpy as jnp
import numpy as np
from jax import lax
from jax.experimental import pallas as pl
from jax.experimental.pallas import tpu as pltpu
from jax.sharding import PartitionSpec as P

AXES = ("slab", "tile")
F32 = jnp.float32
BF16 = jnp.bfloat16
VMEM_LIMIT = 58 * 2**20
SMALL = 16 * 2**20
VM = pl.BlockSpec(memory_space=pltpu.VMEM)
ANY = pl.BlockSpec(memory_space=pl.ANY)
GROUP = 32


def axis_children(offset):
    if offset == -1:
        return ([1], [0])
    if offset == 1:
        return ([0], [1])
    return ([0, 1], [0, 1])


def neighbour_plan():
    plans = []
    for near in np.ndindex(3, 3, 3):
        near = [v - 1 for v in near]
        parts = [axis_children(v) for v in near]
        sources = [(a, b, c) for a in parts[0][0] for b in parts[1][0] for c in parts[2][0]]
        targets = [(a, b, c) for a in parts[0][1] for b in parts[1][1] for c in parts[2][1]]
        taps = []
        for s in sources:
            row = []
            for t in targets:
                o = [2 * near[i] + s[i] - t[i] for i in range(3)]
                row.append(9 * (o[0] + 1) + 3 * (o[1] + 1) + o[2] + 1)
            taps.append(row)
        code = lambda v: 4 * v[0] + 2 * v[1] + v[2]
        plans.append(([code(s) for s in sources], [code(t) for t in targets], taps))
    return plans


PLANS = neighbour_plan()


def tap_block(w_ref, tap):
    return w_ref[tap * 128 : (tap + 1) * 128, :]


def tap_matrix(w_ref, taps):
    return jnp.concatenate(
        [jnp.concatenate([tap_block(w_ref, t) for t in row], axis=1) for row in taps], axis=0
    )


def dot(a, b):
    return jnp.dot(a, b, preferred_element_type=F32)


def add_dots(left, plan, w_ref, total, fresh=False):
    sources, targets, taps = plan
    step = min(2, len(targets))
    for j in range(0, len(targets), step):
        part = dot(left, tap_matrix(w_ref, [row[j : j + step] for row in taps]))
        for k in range(step):
            piece = part[:, k * 128 : (k + 1) * 128]
            if fresh:
                total[targets[j + k]] = piece
            else:
                total[targets[j + k]] += piece


def add_neighbours(idx_ref, w_ref, table, picked, total):
    blocks = total.shape[1]

    def pick(t):
        into = picked[t % 2]
        for first in range(t * blocks, (t + 1) * blocks, GROUP):
            rows = [
                table[pl.ds(pl.multiple_of(idx_ref[first + u], 8), 8), :] for u in range(GROUP)
            ]
            at = (first - t * blocks) * 8
            for u in range(GROUP):
                into[at + u * 8 : at + u * 8 + 8, :] = rows[u]

    for t in range(-1, 26):

        def step(i, carry, t=t):
            if t + 1 < 26:
                pick(t + 1)
            if t >= 0:
                plan = PLANS[t if t < 13 else t + 1]
                near = picked[t % 2]
                left = [near[pl.ds(s, blocks, stride=8), :].astype(BF16) for s in plan[0]]
                add_dots(jnp.concatenate(left, axis=1), plan, w_ref, total)
            return carry

        lax.fori_loop(0, 1, step, 0)


def copies(pairs, sems):
    made = [pltpu.make_async_copy(a, b, sems.at[i]) for i, (a, b) in enumerate(pairs)]
    for copy in made:
        copy.start()
    return made


def fill_table(table, ref, base):
    rows = 128

    def some(i, carry):
        at = pl.ds(pl.multiple_of(i * rows, rows), rows)
        to = pl.multiple_of((base + i * rows) * 8, rows * 8)
        for q in range(8):
            table[pl.ds(to + q, rows, stride=8), :] = (
                ref[at, q * 128 : (q + 1) * 128].astype(F32)
            )
        return carry

    lax.fori_loop(0, ref.shape[0] // rows, some, 0)


def silu(x):
    return x * jax.nn.sigmoid(x)


def home_kernel(sub_ref, coarse_ref, out_ref, place, raw, wide, rows, sems):
    devices = out_ref.shape[0]
    cells = coarse_ref.shape[0]
    part = cells // 4
    spot = pltpu.make_async_copy(sub_ref, place, sems.at[4])
    spot.start()
    loads = copies(
        [(coarse_ref.at[pl.ds(i * part, part)], raw.at[pl.ds(i * part, part)]) for i in range(4)],
        sems,
    )
    for i in range(4):
        loads[i].wait()

        def widen(j, carry, i=i):
            at = pl.ds(pl.multiple_of(i * part + j * 128, 128), 128)
            for half in range(2):
                wide[half, at, :] = raw[at, half * 128 : (half + 1) * 128].astype(F32)
            return carry

        lax.fori_loop(0, part // 128, widen, 0, unroll=2)
    spot.wait()

    def some(i, carry):
        first = i * 32
        k = first // devices
        to = lax.rem(first, devices) * 8 + k
        cells_here = [place[0, first + u] for u in range(32)]
        for half in range(2):
            got = [wide[half, pl.ds(c, 1), :] for c in cells_here]
            for u in range(32):
                rows[half, pl.ds(to + u * 8, 1), :] = got[u]
        return carry

    lax.fori_loop(0, devices * 8 // 32, some, 0)
    for half in range(2):
        out_ref[:, :, half * 128 : (half + 1) * 128] = (
            rows[half].astype(BF16).reshape(devices, 8, 128)
        )


def own_index():
    return lax.axis_index(AXES[0]) * lax.axis_size(AXES[1]) + lax.axis_index(AXES[1])


def roll_kernel(got_ref, home_ref, out_ref):
    devices = got_ref.shape[0]
    me = own_index()
    ids = lax.broadcasted_iota(jnp.int32, (devices, 1), 0)
    lower = jnp.sum(jnp.where(ids < me, got_ref[:, 8:9], 0))
    shift = lax.rem(lower, devices)

    def one(d, carry):
        src = lax.rem(d - shift + devices, devices)
        out_ref[d] = home_ref[src]
        return carry

    lax.fori_loop(0, devices, one, 0, unroll=8)


def select_rows(got_ref, source, scratch, out_ref, done=None):
    devices = got_ref.shape[0]
    blocks, width = source.shape
    lanes = lax.broadcasted_iota(jnp.int32, (devices, blocks), 1)
    pick = jnp.concatenate(
        [(got_ref[:, k : k + 1] == lanes).astype(BF16) for k in range(8)], axis=0
    )
    for c in range(0, width, 256):
        part = dot(pick, source[:, c : c + 256])
        for half in range(2):
            to = scratch.at[half]
            for k in range(8):
                to[pl.ds(k, devices, stride=8), :] = (
                    part[k * devices : (k + 1) * devices, half * 128 : (half + 1) * 128]
                )
            at = c + half * 128
            out_ref[:, :, at : at + 128] = to[...].astype(BF16).reshape(devices, 8, 128)
        if done is not None:
            done(c // 256, pl.ds(c, 256))


def parent_kernel(got_ref, arrived_ref, parent_ref, send_ref, scratch):
    devices = got_ref.shape[0]
    blocks = parent_ref.shape[0]
    me = own_index()
    cols = devices * 8
    home = lax.broadcasted_iota(jnp.int32, (devices, cols), 1) // 8
    row = lax.broadcasted_iota(jnp.int32, (devices, cols), 0)
    counts = got_ref[:, 8:9]
    lower = jnp.sum(jnp.where(row < home, counts, 0), axis=0, keepdims=True)
    upper = jnp.sum(jnp.where(row <= home, counts, 0), axis=0, keepdims=True)
    within = lax.broadcasted_iota(jnp.int32, (1, cols), 1) % 8
    slot = (lower - me + devices - 1) // devices + within
    slot = jnp.where(slot * devices + me < upper, slot, -1)
    pick = (lax.broadcasted_iota(jnp.int32, (blocks, cols), 0) == slot).astype(BF16)
    parent = dot(pick, arrived_ref[...]).astype(BF16)
    parent_ref[...] = parent
    select_rows(got_ref, parent, scratch, send_ref)


def own_kernel(parent_ref, up_ref, w_ref, child_ref, total_ref):
    child_ref[...] = silu(dot(parent_ref[...], up_ref[...])).astype(BF16)
    add_dots(child_ref[...], PLANS[13], w_ref, total_ref, fresh=True)


def own_second_kernel(child_ref, hidden_ref, w_ref, total_ref):
    add_dots(hidden_ref[...], PLANS[13], w_ref, total_ref, fresh=True)
    for q in range(8):
        total_ref[q] += child_ref[:, q * 128 : (q + 1) * 128].astype(F32)


def first_kernel(
    idx_ref, got_ref, child_ref, far_ref, up_ref, w_ref, total_ref,
    hidden_ref, send_ref,
    table, picked, total, idx, w, child, scratch, hidden, send, sems,
):
    blocks = child_ref.shape[0]
    far = far_ref.shape[0]
    rows = 512
    loads = copies(
        [(child_ref, child), (idx_ref, idx), (w_ref, w), (total_ref, total)], sems
    )

    def far_rows(i, carry):
        at = pl.ds(pl.multiple_of(i * rows, rows), rows)
        to = pl.multiple_of((blocks + i * rows) * 8, 8)
        made = silu(dot(far_ref[at, :], up_ref[...])).astype(BF16)
        for q in range(8):
            table[pl.ds(to + q, rows, stride=8), :] = made[:, q * 128 : (q + 1) * 128].astype(F32)
        return carry

    lax.fori_loop(0, far // rows, far_rows, 0)
    last = (blocks + far) * 8
    table[last : last + 8, :] = jnp.zeros((8, 128), F32)
    loads[0].wait()
    fill_table(table, child, 0)
    for load in loads[1:]:
        load.wait()
    add_neighbours(idx, w, table, picked, total)
    for q in range(8):
        hidden[:, q * 128 : (q + 1) * 128] = silu(total[q]).astype(BF16)
    leaving = [pltpu.make_async_copy(hidden, hidden_ref, sems.at[4])]
    leaving[0].start()

    def send_columns(number, columns):
        copy = pltpu.make_async_copy(
            send.at[:, :, columns], send_ref.at[:, :, columns], sems.at[5 + number]
        )
        copy.start()
        leaving.append(copy)

    select_rows(got_ref, hidden, scratch, send, send_columns)
    for copy in leaving:
        copy.wait()


def second_kernel(
    idx_ref, hidden_ref, far_ref, w_ref, total_ref, occ_ref,
    feature_ref, occupancy_ref,
    table, picked, total, idx, w, hidden, far, sems,
):
    blocks = hidden_ref.shape[0]
    rows = far_ref.shape[0]
    half = rows // 2
    loads = copies(
        [
            (hidden_ref, hidden),
            (far_ref.at[pl.ds(0, half)], far.at[pl.ds(0, half)]),
            (far_ref.at[pl.ds(half, half)], far.at[pl.ds(half, half)]),
            (idx_ref, idx),
            (w_ref, w),
            (total_ref, total),
        ],
        sems,
    )
    last = (blocks + rows) * 8
    table[last : last + 8, :] = jnp.zeros((8, 128), F32)
    loads[0].wait()
    fill_table(table, hidden, 0)
    for part in range(2):
        loads[1 + part].wait()
        fill_table(table, far.at[pl.ds(part * half, half)], blocks + part * half)
    for load in loads[3:]:
        load.wait()
    add_neighbours(idx, w, table, picked, total)
    for q in range(8):
        feature_ref[:, q * 128 : (q + 1) * 128] = total[q].astype(BF16)
    lane = lax.broadcasted_iota(jnp.int32, (8, 1024), 1) // 128
    row = lax.broadcasted_iota(jnp.int32, (8, 1024), 0)
    head = jnp.where(lane == row, jnp.concatenate([occ_ref[...].astype(F32)] * 8, axis=1), 0.0)
    occupancy_ref[...] = lax.dot_general(
        head.astype(BF16), feature_ref[...], (((1,), (1,)), ((), ())), preferred_element_type=F32
    )


def shape(*dims, dtype=BF16):
    return jax.ShapeDtypeStruct(dims, dtype)


def call(kernel, out_shape, in_specs, scratch=(), out_specs=None, flops=0, limit=VMEM_LIMIT):
    return pl.pallas_call(
        kernel,
        out_shape=out_shape,
        in_specs=in_specs,
        out_specs=out_specs or jax.tree.map(lambda _: VM, out_shape),
        scratch_shapes=list(scratch),
        compiler_params=pltpu.CompilerParams(vmem_limit_bytes=limit),
        cost_estimate=pl.CostEstimate(flops=flops, bytes_accessed=4 * 2**20, transcendentals=0),
    )


def exchange(x):
    return lax.all_to_all(x, AXES, split_axis=0, concat_axis=0, tiled=True)


def body(
    coarse, counts, subdivided, requested, neighbours,
    up_weight, first_conv, second_conv, occupancy_weight,
):
    devices = lax.axis_size(AXES)
    blocks = neighbours.shape[1]
    far = devices * 8
    table_rows = (blocks + far + 8) * 8

    note = jnp.concatenate(
        [requested[0], jnp.broadcast_to(counts[:, None], (devices, 8))], axis=1
    )
    got = exchange(note.reshape(devices, 1, 16)).reshape(devices, 16)
    cells, width = coarse.shape
    home = call(
        home_kernel,
        shape(devices, 8, width),
        [ANY, ANY],
        [
            pltpu.SMEM(subdivided.shape, jnp.int32),
            pltpu.VMEM((cells, width), BF16),
            pltpu.VMEM((2, cells, 128), F32),
            pltpu.VMEM((2, far, 128), F32),
            pltpu.SemaphoreType.DMA((5,)),
        ],
        flops=2**30,
    )(subdivided, coarse)
    idx = (neighbours * 8).reshape(-1)

    leaving = call(roll_kernel, shape(devices, 8, 256), [VM, VM], limit=SMALL)(got, home)
    arrived = exchange(leaving)
    parent, send = call(
        parent_kernel,
        (shape(blocks, 256), shape(devices, 8, 256)),
        [VM, VM],
        [pltpu.VMEM((2, far, 128), F32)],
        limit=SMALL,
    )(got, arrived.reshape(far, 256))
    far_parent = exchange(send).reshape(far, 256)

    work = [
        pltpu.VMEM((table_rows, 128), F32),
        (pltpu.VMEM((blocks * 8, 128), F32),) * 2,
        pltpu.VMEM((8, blocks, 128), F32),
        pltpu.SMEM(idx.shape, jnp.int32),
        pltpu.VMEM(first_conv.shape, BF16),
        pltpu.VMEM((blocks, 1024), BF16),
    ]
    own = shape(8, blocks, 128, dtype=F32)
    child, total = call(own_kernel, (shape(blocks, 1024), own), [VM] * 3, flops=3 * 2**30, limit=SMALL)(
        parent, up_weight, first_conv
    )
    hidden, send = call(
        first_kernel,
        (shape(blocks, 1024), shape(devices, 8, 1024)),
        [ANY, VM, ANY, VM, VM, ANY, ANY],
        work
        + [
            pltpu.VMEM((2, far, 128), F32),
            pltpu.VMEM((blocks, 1024), BF16),
            pltpu.VMEM((devices, 8, 1024), BF16),
            pltpu.SemaphoreType.DMA((9,)),
        ],
        (ANY, ANY),
    )(idx, got, child, far_parent, up_weight, first_conv, total)
    far_hidden = exchange(send).reshape(far, 1024)
    total = call(own_second_kernel, own, [VM] * 3, flops=3 * 2**30, limit=SMALL)(child, hidden, second_conv)
    return tuple(
        call(
            second_kernel,
            (shape(blocks, 1024), shape(8, blocks, dtype=F32)),
            [ANY] * 5 + [VM],
            work + [pltpu.VMEM((far, 1024), BF16), pltpu.SemaphoreType.DMA((6,))],
        )(idx, hidden, far_hidden, second_conv, total, occupancy_weight.reshape(1, 128))
    )


def solution(mesh):
    rows = P(AXES, None)
    in_specs = (rows, P(AXES), rows, P(AXES, None, None), P(None, AXES), P(), P(), P(), P())
    out_specs = (rows, P(None, AXES))
    return jax.shard_map(body, mesh=mesh, in_specs=in_specs, out_specs=out_specs, check_vma=False)
```

time: 148 us -> 136 us (0.919)
  blocking collectives: 58.3 us -> 18.6 us
  waiting for transfers between devices: 14.3 us -> 41.6 us
  starting transfers between devices: 16 us -> 21.6 us
  local copies, waits for them, and re-layouts: 11.7 us -> 7.57 us
    all_to_all x2 -> x1, blocking collectives: 58.3 us -> 18.6 us  [exchange(): return lax.all_to_all(x, AXES, split_axis=0, concat_axis=0, tiled=True)]
    all_to_all x2 -> x3, waiting for transfers between devices: 14.3 us -> 41.6 us  [exchange(): return lax.all_to_all(x, AXES, split_axis=0, concat_axis=0, tiled=True)]
    gather x1 -> x0, local copies, waits for them, and re-layouts: 7.37 us -> none  [body(): home = coarse[order].reshape(devices, 8, -1)]
    all_to_all x2 -> x3, starting transfers between devices: 16 us -> 21.6 us  [exchange(): return lax.all_to_all(x, AXES, split_axis=0, concat_axis=0, tiled=True)]
    unnamed x7 -> x25, local copies, waits for them, and re-layouts: 2.21 us -> 6.31 us
    pallas_call x1, Pallas kernels: 18.3 us -> 16.4 us  [body(): call(second_kernel, (shape(blocks, 1024), shape(8, blocks, dtype=F32)), [...]
    pallas_call x3 -> x6, Pallas kernels: 27.1 us -> 28.7 us  [the longest x1 18.4 us: body(): call(first_kernel, (shape(blocks, 1024), shape(devices, 8, 1024)), [ANY,...]
  transfers between devices with their start and end apart: 2 -> 3, of which waited for: 2 -> 3; matrix products, arithmetic and copies ran while one was open for 6% -> 0% of each run, Pallas kernels for 0% -> 6%
where the time goes in v2:
time: 136 us
  Pallas kernels  45.1 us (33%)
  waiting for transfers between devices  41.6 us (31%)
  starting transfers between devices  21.6 us (16%)
  blocking collectives  18.6 us (14%)
  local copies, waits for them, and re-layouts  7.57 us (6%)
  between operations  1.64 us (1%)
    all_to_all x3, waiting for transfers between devices, exchange(): return lax.all_to_all(x, AXES, split_axis=0, concat_axis=0, tiled=True)  41.6 us
    all_to_all x3, starting transfers between devices, exchange(): return lax.all_to_all(x, AXES, split_axis=0, concat_axis=0, tiled=True)  21.6 us
    all_to_all x1, blocking collectives, exchange(): return lax.all_to_all(x, AXES, split_axis=0, concat_axis=0, tiled=True)  18.6 us
    pallas_call x1, Pallas kernels, body(): call(first_kernel, (shape(blocks, 1024), shape(devices, 8, 1024)), [ANY,...  18.4 us
    pallas_call x1, Pallas kernels, body(): call(second_kernel, (shape(blocks, 1024), shape(8, blocks, dtype=F32)), [...  16.4 us
    unnamed x25, local copies, waits for them, and re-layouts  6.31 us
    pallas_call x1, Pallas kernels, body(): call(home_kernel, shape(devices, 8, width), [ANY, ANY], [pltpu.SMEM(subdi...  4.72 us
  transfers between devices with their start and end apart: 3, of which 3 were waited for; matrix products, arithmetic and copies ran while one was open for 0% of the time, Pallas kernels for 6%

profile of v2, /device:TPU:1, one launch (start us, length us, event | category | flops | bytes accessed | tf_op | source)
XLA Modules:
  0.0 136.1 jit_solution(10724398157496361229)
XLA Ops:
  1.3 0.8 copy.12
  2.1 0.6 concatenate.3
  2.7 11.5 %all-to-all-start = ((s32[128,1,16]{2,1,0:T(1,128)}), s32[128,1,16]{2,1,0:T(1,128)S(1)}, u32[]{:S(2)}, u32[]{:S(2)}) async-start(s32[128,1,16]{2,1,0:T(1,128)} %bitcast.2), calls=%async_computation | async-start | bytes 131072 | tf_op jit(solution)/shard_map/all_to_all | solution.py:343
  14.2 0.0 copy-start.11
  14.2 0.0 copy-start.7
  14.2 4.7 %shard_map.104.home_ref = bf16[128,8,256]{2,1,0:T(8,128)(2,1)} custom-call(s32[1,1024]{1,0:T(1,128)} %sub_ref.1, bf16[8192,256]{1,0:T(8,128)(2,1)} %coarse_ref.1), custom_call_target="tpu_custom_call" | custom-call | flops 1073741824 | bytes 4194304 | tf_op jit(solution)/shard_map/pallas_call | solution.py:360
  19.0 4.7 %all-to-all-done = s32[128,1,16]{2,1,0:T(1,128)S(1)} async-done(((s32[128,1,16]{2,1,0:T(1,128)}), s32[128,1,16]{2,1,0:T(1,128)S(1)}, u32[]{:S(2)}, u32[]{:S(2)}) %all-to-all-start) | async-done | bytes 8224 | tf_op jit(solution)/shard_map/all_to_all | solution.py:343
  23.7 1.1 copy-done.2
  24.7 0.6 shard_map.105
  25.3 18.6 %all_to_all.20 = bf16[128,8,256]{2,1,0:T(8,128)(2,1)S(1)} all-to-all(bf16[128,8,256]{2,1,0:T(8,128)(2,1)S(1)} %shard_map.105), channel_id=1, replica_groups=mesh['slab'=4,'tile'=32] {'slab','tile'}, dimensions={0} | all-to-all | bytes 1048576 | tf_op jit(solution)/shard_map/all_to_all | solution.py:343
  43.9 2.2 %shard_map.106 = (bf16[512,256]{1,0:T(8,128)(2,1)S(1)}, bf16[128,8,256]{2,1,0:T(8,128)(2,1)}) custom-call(s32[128,16]{1,0:T(8,128)S(1)} %bitcast.11, bf16[1024,256]{1,0:T(8,128)(2,1)S(1)} %bitcast.9), custom_call_target="tpu_custom_call" | custom-call | bytes 4194304 | tf_op jit(solution)/shard_map/pallas_call | solution.py:377
  46.2 4.5 %all-to-all-start.2 = ((bf16[128,8,256]{2,1,0:T(8,128)(2,1)}), bf16[128,8,256]{2,1,0:T(8,128)(2,1)S(1)}, u32[]{:S(2)}, u32[]{:S(2)}) async-start(bf16[128,8,256]{2,1,0:T(8,128)(2,1)} %get-tuple-element.10), calls=%async_computation.2 | async-start | bytes 1048576 | tf_op jit(solution)/shard_map/all_to_all | solution.py:343
  50.7 0.6 reshape.26.idx_ref
  51.4 1.5 %shard_map.107 = (bf16[512,1024]{1,0:T(8,128)(2,1)S(1)}, f32[8,512,128]{2,1,0:T(8,128)S(1)}) custom-call(bf16[512,256]{1,0:T(8,128)(2,1)S(1)} %get-tuple-element.8.parent_ref, bf16[256,1024]{1,0:T(8,128)(2,1)S(1)} %copy-done.9, bf16[3456,128]{1,0:T(8,128)(2,1)S(1)} %copy-done.7), custom_call_target="tpu_custom_call" | custom-call | flops 3221225472 | bytes 4194304 | tf_op jit(solution)/shard_map/pallas_call | solution.py:395
  52.9 1.3 copy-done
  54.2 1.0 copy-done.4
  55.2 9.2 %all-to-all-done.2 = bf16[128,8,256]{2,1,0:T(8,128)(2,1)S(1)} async-done(((bf16[128,8,256]{2,1,0:T(8,128)(2,1)}), bf16[128,8,256]{2,1,0:T(8,128)(2,1)S(1)}, u32[]{:S(2)}, u32[]{:S(2)}) %all-to-all-start.2) | async-done | bytes 524320 | tf_op jit(solution)/shard_map/all_to_all | solution.py:343
  64.4 0.8 copy-done.10
  65.2 18.4 %shard_map.108 = (bf16[512,1024]{1,0:T(8,128)(2,1)}, bf16[128,8,1024]{2,1,0:T(8,128)(2,1)}) custom-call(s32[13312]{0:T(1024)} %reshape.26.idx_ref, s32[128,16]{1,0:T(8,128)} %bitcast.12, bf16[512,1024]{1,0:T(8,128)(2,1)} %copy-done.4, bf16[1024,256]{1,0:T(8,128)(2,1)} %bitcast.13, bf16[256,1024]{1,0:T(8,128)(2,1)} %up_ref.3, bf16[3456,128]{1,0:T(8,128)(2,1)} %w_ref.5, ...), custom_call_target="tpu_custom_call" | custom-call | bytes 4194304 | tf_op jit(solution)/shard_map/pallas_call | solution.py:398
  83.7 5.6 %all-to-all-start.3 = ((bf16[128,8,1024]{2,1,0:T(8,128)(2,1)}), bf16[128,8,1024]{2,1,0:T(8,128)(2,1)}, u32[]{:S(2)}, u32[]{:S(2)}) async-start(bf16[128,8,1024]{2,1,0:T(8,128)(2,1)} %get-tuple-element.13), calls=%async_computation.3 | async-start | bytes 4194304 | tf_op jit(solution)/shard_map/all_to_all | solution.py:343
  89.3 1.3 shard_map.109.total_ref
  90.5 1.3 copy-done.1
  91.9 27.7 %all-to-all-done.3 = bf16[128,8,1024]{2,1,0:T(8,128)(2,1)} async-done(((bf16[128,8,1024]{2,1,0:T(8,128)(2,1)}), bf16[128,8,1024]{2,1,0:T(8,128)(2,1)}, u32[]{:S(2)}, u32[]{:S(2)}) %all-to-all-start.3) | async-done | bytes 2097184 | tf_op jit(solution)/shard_map/all_to_all | solution.py:343
  119.6 16.4 %shard_map.110 = (bf16[512,1024]{1,0:T(8,128)(2,1)}, f32[8,512]{1,0:T(8,128)}) custom-call(s32[13312]{0:T(1024)} %reshape.26.idx_ref, bf16[512,1024]{1,0:T(8,128)(2,1)} %get-tuple-element.12.hidden_ref, bf16[1024,1024]{1,0:T(8,128)(2,1)} %bitcast.6.far_ref, bf16[3456,128]{1,0:T(8,128)(2,1)} %w_ref.7, f32[8,512,128]{2,1,0:T(8,128)} %copy-done.1, ...), custom_call_target="tpu_custom_call" | custom-call | bytes 4194304 | tf_op jit(solution)/shard_map/pallas_call | solution.py:414
  (18 shorter events, 0.0 us)
Async XLA Ops:
  2.7 21.0 %all-to-all-start = ((s32[128,1,16]{2,1,0:T(1,128)}), s32[128,1,16]{2,1,0:T(1,128)S(1)}, u32[]{:S(2)}, u32[]{:S(2)}) async-start(s32[128,1,16]{2,1,0:T(1,128)} %bitcast.2), calls=%async_computation | async-start | bytes 131072 | tf_op jit(solution)/shard_map/all_to_all | solution.py:343
  14.2 36.5 %copy-start.11 = (s32[26,512]{1,0:T(8,128)S(1)}, s32[26,512]{1,0:T(8,128)}, u32[]{:S(2)}) copy-start(s32[26,512]{1,0:T(8,128)} %param.13) | copy-start | bytes 159748
  14.2 37.1 %copy-start.7 = (bf16[3456,128]{1,0:T(8,128)(2,1)S(1)}, bf16[3456,128]{1,0:T(8,128)(2,1)}, u32[]{:S(2)}) copy-start(bf16[3456,128]{1,0:T(8,128)(2,1)} %w_ref.5) | copy-start | bytes 2654212
  14.2 37.1 %copy-start.9 = (bf16[256,1024]{1,0:T(8,128)(2,1)S(1)}, bf16[256,1024]{1,0:T(8,128)(2,1)}, u32[]{:S(2)}) copy-start(bf16[256,1024]{1,0:T(8,128)(2,1)} %up_ref.3) | copy-start | bytes 1572868
  23.7 29.2 %copy-start.3 = (s32[128,1,16]{2,1,0:T(1,128)}, s32[128,1,16]{2,1,0:T(1,128)S(1)}, u32[]{:S(2)}) copy-start(s32[128,1,16]{2,1,0:T(1,128)S(1)} %all-to-all-done) | copy-start | bytes 24580
  23.7 1.1 copy-start.2
  46.2 18.2 %all-to-all-start.2 = ((bf16[128,8,256]{2,1,0:T(8,128)(2,1)}), bf16[128,8,256]{2,1,0:T(8,128)(2,1)S(1)}, u32[]{:S(2)}, u32[]{:S(2)}) async-start(bf16[128,8,256]{2,1,0:T(8,128)(2,1)} %get-tuple-element.10), calls=%async_computation.2 | async-start | bytes 1048576 | tf_op jit(solution)/shard_map/all_to_all | solution.py:343
  52.9 1.3 copy-start
  54.2 1.0 copy-start.4
  64.4 0.8 copy-start.10
  83.7 5.6 %copy-start.5 = (bf16[512,1024]{1,0:T(8,128)(2,1)S(1)}, bf16[512,1024]{1,0:T(8,128)(2,1)}, u32[]{:S(2)}) copy-start(bf16[512,1024]{1,0:T(8,128)(2,1)} %copy-done.4) | copy-start | bytes 3145732
  83.7 5.6 %copy-start.6 = (bf16[512,1024]{1,0:T(8,128)(2,1)S(1)}, bf16[512,1024]{1,0:T(8,128)(2,1)}, u32[]{:S(2)}) copy-start(bf16[512,1024]{1,0:T(8,128)(2,1)} %get-tuple-element.12.hidden_ref) | copy-start | bytes 3145732
  83.7 5.6 %copy-start.8 = (bf16[3456,128]{1,0:T(8,128)(2,1)S(1)}, bf16[3456,128]{1,0:T(8,128)(2,1)}, u32[]{:S(2)}) copy-start(bf16[3456,128]{1,0:T(8,128)(2,1)} %w_ref.7) | copy-start | bytes 2654212
  83.7 35.9 %all-to-all-start.3 = ((bf16[128,8,1024]{2,1,0:T(8,128)(2,1)}), bf16[128,8,1024]{2,1,0:T(8,128)(2,1)}, u32[]{:S(2)}, u32[]{:S(2)}) async-start(bf16[128,8,1024]{2,1,0:T(8,128)(2,1)} %get-tuple-element.13), calls=%async_computation.3 | async-start | bytes 4194304 | tf_op jit(solution)/shard_map/all_to_all | solution.py:343
  90.5 1.4 copy-start.1

commit v3 on v2

--- a/solution.py
+++ b/solution.py
@@ -126,7 +126,8 @@
 
 
 def silu(x):
-    return x * jax.nn.sigmoid(x)
+    half = 0.5 * x
+    return half + half * jnp.tanh(half)
 
 
 def home_kernel(sub_ref, coarse_ref, out_ref, place, raw, wide, rows, sems):
@@ -369,6 +370,7 @@
             pltpu.SemaphoreType.DMA((5,)),
         ],
         flops=2**30,
+        limit=SMALL + 8 * 2**20,
     )(subdivided, coarse)
     idx = (neighbours * 8).reshape(-1)
 
@@ -407,6 +409,7 @@
             pltpu.SemaphoreType.DMA((9,)),
         ],
         (ANY, ANY),
+        limit=52 * 2**20,
     )(idx, got, child, far_parent, up_weight, first_conv, total)
     far_hidden = exchange(send).reshape(far, 1024)
     total = call(own_second_kernel, own, [VM] * 3, flops=3 * 2**30, limit=SMALL)(child, hidden, second_conv)

time: 136 us -> 134 us (0.985)
  Pallas kernels: 45.1 us -> 41.8 us
    pallas_call x1, Pallas kernels: 4.72 us -> 2.42 us  [body(): call(home_kernel, shape(devices, 8, width), [ANY, ANY], [pltpu.SMEM(subdi...]
  transfers between devices with their start and end apart: 3 -> 3, of which waited for: 3 -> 3; matrix products, arithmetic and copies ran while one was open for 0% -> 0% of each run, Pallas kernels for 6% -> 4%
where the time goes in v3:
time: 134 us
  Pallas kernels  41.8 us (31%)
  waiting for transfers between devices  41.4 us (31%)
  starting transfers between devices  21.6 us (16%)
  blocking collectives  19.2 us (14%)
  local copies, waits for them, and re-layouts  7.99 us (6%)
  between operations  1.67 us (1%)
    all_to_all x3, waiting for transfers between devices, exchange(): return lax.all_to_all(x, AXES, split_axis=0, concat_axis=0, tiled=True)  41.4 us
    all_to_all x3, starting transfers between devices, exchange(): return lax.all_to_all(x, AXES, split_axis=0, concat_axis=0, tiled=True)  21.6 us
    all_to_all x1, blocking collectives, exchange(): return lax.all_to_all(x, AXES, split_axis=0, concat_axis=0, tiled=True)  19.2 us
    pallas_call x1, Pallas kernels, body(): call(first_kernel, (shape(blocks, 1024), shape(devices, 8, 1024)), [ANY,...  17.3 us
    pallas_call x1, Pallas kernels, body(): call(second_kernel, (shape(blocks, 1024), shape(8, blocks, dtype=F32)), [...  16.4 us
    unnamed x25, local copies, waits for them, and re-layouts  7.35 us
  transfers between devices with their start and end apart: 3, of which 3 were waited for; matrix products, arithmetic and copies ran while one was open for 0% of the time, Pallas kernels for 4%

profile of v3, /device:TPU:1, one launch (start us, length us, event | category | flops | bytes accessed | tf_op | source)
XLA Modules:
  0.0 133.7 jit_solution(4448518222185490574)
XLA Ops:
  1.3 0.8 copy.12
  2.1 0.6 concatenate.3
  2.7 11.5 %all-to-all-start = ((s32[128,1,16]{2,1,0:T(1,128)}), s32[128,1,16]{2,1,0:T(1,128)S(1)}, u32[]{:S(2)}, u32[]{:S(2)}) async-start(s32[128,1,16]{2,1,0:T(1,128)} %bitcast.2), calls=%async_computation | async-start | bytes 131072 | tf_op jit(solution)/shard_map/all_to_all | solution.py:344
  14.2 0.0 copy-start
  14.2 2.2 %copy-done = bf16[8192,256]{1,0:T(8,128)(2,1)S(1)} copy-done((bf16[8192,256]{1,0:T(8,128)(2,1)S(1)}, bf16[8192,256]{1,0:T(8,128)(2,1)}, u32[]{:S(2)}) %copy-start) | copy-done | bytes 4194328
  16.4 0.7 copy-done.10
  17.1 2.4 %shard_map.104.home_ref = bf16[128,8,256]{2,1,0:T(8,128)(2,1)S(1)} custom-call(s32[1,1024]{1,0:T(1,128)S(1)} %copy-done.10, bf16[8192,256]{1,0:T(8,128)(2,1)S(1)} %copy-done), custom_call_target="tpu_custom_call" | custom-call | flops 1073741824 | bytes 4194304 | tf_op jit(solution)/shard_map/pallas_call | solution.py:361
  19.5 0.0 copy-start.11
  19.5 0.0 copy-start.8
  19.5 4.1 %all-to-all-done = s32[128,1,16]{2,1,0:T(1,128)S(1)} async-done(((s32[128,1,16]{2,1,0:T(1,128)}), s32[128,1,16]{2,1,0:T(1,128)S(1)}, u32[]{:S(2)}, u32[]{:S(2)}) %all-to-all-start) | async-done | bytes 8224 | tf_op jit(solution)/shard_map/all_to_all | solution.py:344
  23.6 0.6 shard_map.105
  24.2 19.2 %all_to_all.20 = bf16[128,8,256]{2,1,0:T(8,128)(2,1)S(1)} all-to-all(bf16[128,8,256]{2,1,0:T(8,128)(2,1)S(1)} %shard_map.105), channel_id=1, replica_groups=mesh['slab'=4,'tile'=32] {'slab','tile'}, dimensions={0} | all-to-all | bytes 1048576 | tf_op jit(solution)/shard_map/all_to_all | solution.py:344
  43.5 2.2 %shard_map.106 = (bf16[512,256]{1,0:T(8,128)(2,1)S(1)}, bf16[128,8,256]{2,1,0:T(8,128)(2,1)}) custom-call(s32[128,16]{1,0:T(8,128)S(1)} %bitcast.12, bf16[1024,256]{1,0:T(8,128)(2,1)S(1)} %bitcast.10), custom_call_target="tpu_custom_call" | custom-call | bytes 4194304 | tf_op jit(solution)/shard_map/pallas_call | solution.py:379
  45.7 4.5 %all-to-all-start.2 = ((bf16[128,8,256]{2,1,0:T(8,128)(2,1)}), bf16[128,8,256]{2,1,0:T(8,128)(2,1)S(1)}, u32[]{:S(2)}, u32[]{:S(2)}) async-start(bf16[128,8,256]{2,1,0:T(8,128)(2,1)} %get-tuple-element.10), calls=%async_computation.2 | async-start | bytes 1048576 | tf_op jit(solution)/shard_map/all_to_all | solution.py:344
  50.3 1.7 %shard_map.107 = (bf16[512,1024]{1,0:T(8,128)(2,1)S(1)}, f32[8,512,128]{2,1,0:T(8,128)S(1)}) custom-call(bf16[512,256]{1,0:T(8,128)(2,1)S(1)} %get-tuple-element.8.parent_ref, bf16[256,1024]{1,0:T(8,128)(2,1)S(1)} %copy-done.8, bf16[3456,128]{1,0:T(8,128)(2,1)S(1)} %copy-done.6), custom_call_target="tpu_custom_call" | custom-call | flops 3221225472 | bytes 4194304 | tf_op jit(solution)/shard_map/pallas_call | solution.py:397
  52.0 1.3 copy-done.1
  53.3 1.0 copy-done.3
  54.3 9.6 %all-to-all-done.2 = bf16[128,8,256]{2,1,0:T(8,128)(2,1)S(1)} async-done(((bf16[128,8,256]{2,1,0:T(8,128)(2,1)}), bf16[128,8,256]{2,1,0:T(8,128)(2,1)S(1)}, u32[]{:S(2)}, u32[]{:S(2)}) %all-to-all-start.2) | async-done | bytes 524320 | tf_op jit(solution)/shard_map/all_to_all | solution.py:344
  63.9 17.3 %shard_map.108 = (bf16[512,1024]{1,0:T(8,128)(2,1)}, bf16[128,8,1024]{2,1,0:T(8,128)(2,1)}) custom-call(s32[13312]{0:T(1024)S(1)} %reshape.26.idx_ref, s32[128,16]{1,0:T(8,128)S(1)} %bitcast.13, bf16[512,1024]{1,0:T(8,128)(2,1)} %copy-done.3, bf16[1024,256]{1,0:T(8,128)(2,1)S(1)} %bitcast.9, bf16[256,1024]{1,0:T(8,128)(2,1)S(1)} %copy-done.8, ...), custom_call_target="tpu_custom_call" | custom-call | bytes 4194304 | tf_op jit(solution)/shard_map/pallas_call | solution.py:400
  81.2 5.6 %all-to-all-start.3 = ((bf16[128,8,1024]{2,1,0:T(8,128)(2,1)}), bf16[128,8,1024]{2,1,0:T(8,128)(2,1)}, u32[]{:S(2)}, u32[]{:S(2)}) async-start(bf16[128,8,1024]{2,1,0:T(8,128)(2,1)} %get-tuple-element.13), calls=%async_computation.3 | async-start | bytes 4194304 | tf_op jit(solution)/shard_map/all_to_all | solution.py:344
  86.9 1.3 shard_map.109.total_ref
  88.2 1.3 %copy-done.2 = f32[8,512,128]{2,1,0:T(8,128)} copy-done((f32[8,512,128]{2,1,0:T(8,128)}, f32[8,512,128]{2,1,0:T(8,128)S(1)}, u32[]{:S(2)}) %copy-start.2) | copy-done | bytes 2097176
  89.5 27.7 %all-to-all-done.3 = bf16[128,8,1024]{2,1,0:T(8,128)(2,1)} async-done(((bf16[128,8,1024]{2,1,0:T(8,128)(2,1)}), bf16[128,8,1024]{2,1,0:T(8,128)(2,1)}, u32[]{:S(2)}, u32[]{:S(2)}) %all-to-all-start.3) | async-done | bytes 2097184 | tf_op jit(solution)/shard_map/all_to_all | solution.py:344
  117.2 16.4 %shard_map.110 = (bf16[512,1024]{1,0:T(8,128)(2,1)}, f32[8,512]{1,0:T(8,128)}) custom-call(s32[13312]{0:T(1024)} %copy-done.9, bf16[512,1024]{1,0:T(8,128)(2,1)} %get-tuple-element.12.hidden_ref, bf16[1024,1024]{1,0:T(8,128)(2,1)} %bitcast.6.far_ref, bf16[3456,128]{1,0:T(8,128)(2,1)} %w_ref.7, f32[8,512,128]{2,1,0:T(8,128)} %copy-done.2, bf16[1,128]{1,0:T(2,128)(2,1)} %bitcast.15), custom_call_target="tpu_custom_call" | custom-call | bytes 4194304 | tf_op jit(solution)/shard_map/pallas_call | solution.py:417
  (18 shorter events, 0.1 us)
Async XLA Ops:
  2.7 20.9 %all-to-all-start = ((s32[128,1,16]{2,1,0:T(1,128)}), s32[128,1,16]{2,1,0:T(1,128)S(1)}, u32[]{:S(2)}, u32[]{:S(2)}) async-start(s32[128,1,16]{2,1,0:T(1,128)} %bitcast.2), calls=%async_computation | async-start | bytes 131072 | tf_op jit(solution)/shard_map/all_to_all | solution.py:344
  14.2 2.2 %copy-start = (bf16[8192,256]{1,0:T(8,128)(2,1)S(1)}, bf16[8192,256]{1,0:T(8,128)(2,1)}, u32[]{:S(2)}) copy-start(bf16[8192,256]{1,0:T(8,128)(2,1)} %coarse_ref.1) | copy-start | bytes 12582916
  16.4 0.7 copy-start.10
  19.5 30.7 %copy-start.11 = (s32[26,512]{1,0:T(8,128)S(1)}, s32[26,512]{1,0:T(8,128)}, u32[]{:S(2)}) copy-start(s32[26,512]{1,0:T(8,128)} %param.13) | copy-start | bytes 159748
  19.5 30.7 %copy-start.6 = (bf16[3456,128]{1,0:T(8,128)(2,1)S(1)}, bf16[3456,128]{1,0:T(8,128)(2,1)}, u32[]{:S(2)}) copy-start(bf16[3456,128]{1,0:T(8,128)(2,1)} %w_ref.5) | copy-start | bytes 2654212
  19.5 30.7 %copy-start.8 = (bf16[256,1024]{1,0:T(8,128)(2,1)S(1)}, bf16[256,1024]{1,0:T(8,128)(2,1)}, u32[]{:S(2)}) copy-start(bf16[256,1024]{1,0:T(8,128)(2,1)} %up_ref.3) | copy-start | bytes 1572868
  45.7 18.2 %all-to-all-start.2 = ((bf16[128,8,256]{2,1,0:T(8,128)(2,1)}), bf16[128,8,256]{2,1,0:T(8,128)(2,1)S(1)}, u32[]{:S(2)}, u32[]{:S(2)}) async-start(bf16[128,8,256]{2,1,0:T(8,128)(2,1)} %get-tuple-element.10), calls=%async_computation.2 | async-start | bytes 1048576 | tf_op jit(solution)/shard_map/all_to_all | solution.py:344
  50.2 13.7 %copy-start.9 = (s32[13312]{0:T(1024)}, s32[13312]{0:T(1024)S(1)}, u32[]{:S(2)}) copy-start(s32[13312]{0:T(1024)S(1)} %reshape.26.idx_ref) | copy-start | bytes 159748
  52.0 1.3 %copy-start.1 = (f32[8,512,128]{2,1,0:T(8,128)}, f32[8,512,128]{2,1,0:T(8,128)S(1)}, u32[]{:S(2)}) copy-start(f32[8,512,128]{2,1,0:T(8,128)S(1)} %get-tuple-element.11.total_ref) | copy-start | bytes 6291460
  53.3 1.0 copy-start.3
  81.2 5.7 %copy-start.4 = (bf16[512,1024]{1,0:T(8,128)(2,1)S(1)}, bf16[512,1024]{1,0:T(8,128)(2,1)}, u32[]{:S(2)}) copy-start(bf16[512,1024]{1,0:T(8,128)(2,1)} %copy-done.3) | copy-start | bytes 3145732
  81.2 5.7 %copy-start.5 = (bf16[512,1024]{1,0:T(8,128)(2,1)S(1)}, bf16[512,1024]{1,0:T(8,128)(2,1)}, u32[]{:S(2)}) copy-start(bf16[512,1024]{1,0:T(8,128)(2,1)} %get-tuple-element.12.hidden_ref) | copy-start | bytes 3145732
  81.2 5.7 %copy-start.7 = (bf16[3456,128]{1,0:T(8,128)(2,1)S(1)}, bf16[3456,128]{1,0:T(8,128)(2,1)}, u32[]{:S(2)}) copy-start(bf16[3456,128]{1,0:T(8,128)(2,1)} %w_ref.7) | copy-start | bytes 2654212
  81.2 35.9 %all-to-all-start.3 = ((bf16[128,8,1024]{2,1,0:T(8,128)(2,1)}), bf16[128,8,1024]{2,1,0:T(8,128)(2,1)}, u32[]{:S(2)}, u32[]{:S(2)}) async-start(bf16[128,8,1024]{2,1,0:T(8,128)(2,1)} %get-tuple-element.13), calls=%async_computation.3 | async-start | bytes 4194304 | tf_op jit(solution)/shard_map/all_to_all | solution.py:344
  88.2 1.4 %copy-start.2 = (f32[8,512,128]{2,1,0:T(8,128)}, f32[8,512,128]{2,1,0:T(8,128)S(1)}, u32[]{:S(2)}) copy-start(f32[8,512,128]{2,1,0:T(8,128)S(1)} %shard_map.109.total_ref) | copy-start | bytes 6291460

commit v4 on v3

--- a/solution.py
+++ b/solution.py
@@ -75,7 +75,7 @@
                 total[targets[j + k]] += piece
 
 
-def add_neighbours(idx_ref, w_ref, table, picked, total):
+def add_neighbours(idx_ref, w_ref, table, picked, total, late=()):
     blocks = total.shape[1]
 
     def pick(t):
@@ -101,6 +101,9 @@
             return carry
 
         lax.fori_loop(0, 1, step, 0)
+        if t < 0:
+            for load in late:
+                load.wait()
 
 
 def copies(pairs, sems):
@@ -292,28 +295,25 @@
 ):
     blocks = hidden_ref.shape[0]
     rows = far_ref.shape[0]
-    half = rows // 2
-    loads = copies(
-        [
-            (hidden_ref, hidden),
-            (far_ref.at[pl.ds(0, half)], far.at[pl.ds(0, half)]),
-            (far_ref.at[pl.ds(half, half)], far.at[pl.ds(half, half)]),
-            (idx_ref, idx),
-            (w_ref, w),
-            (total_ref, total),
-        ],
-        sems,
-    )
+    part = rows // 4
+    parts = [pl.ds(i * part, part) for i in range(4)]
+    pairs = [(hidden_ref, hidden)] + [(far_ref.at[at], far.at[at]) for at in parts]
+    loads = copies(pairs + [(idx_ref, idx)], sems)
+    late = [
+        pltpu.make_async_copy(w_ref, w, sems.at[6]),
+        pltpu.make_async_copy(total_ref, total, sems.at[7]),
+    ]
+    for load in late:
+        load.start()
     last = (blocks + rows) * 8
     table[last : last + 8, :] = jnp.zeros((8, 128), F32)
     loads[0].wait()
     fill_table(table, hidden, 0)
-    for part in range(2):
-        loads[1 + part].wait()
-        fill_table(table, far.at[pl.ds(part * half, half)], blocks + part * half)
-    for load in loads[3:]:
-        load.wait()
-    add_neighbours(idx, w, table, picked, total)
+    for i in range(4):
+        loads[1 + i].wait()
+        fill_table(table, far.at[parts[i]], blocks + i * part)
+    loads[5].wait()
+    add_neighbours(idx, w, table, picked, total, late)
     for q in range(8):
         feature_ref[:, q * 128 : (q + 1) * 128] = total[q].astype(BF16)
     lane = lax.broadcasted_iota(jnp.int32, (8, 1024), 1) // 128
@@ -418,7 +418,11 @@
             second_kernel,
             (shape(blocks, 1024), shape(8, blocks, dtype=F32)),
             [ANY] * 5 + [VM],
-            work + [pltpu.VMEM((far, 1024), BF16), pltpu.SemaphoreType.DMA((6,))],
+            work
+            + [
+                pltpu.VMEM((far, 1024), BF16),
+                pltpu.SemaphoreType.DMA((8,)),
+            ],
         )(idx, hidden, far_hidden, second_conv, total, occupancy_weight.reshape(1, 128))
     )
 

time: 134 us -> 134 us (level)
  no operation moved by 1% of the time
where the time goes in v4:
time: 134 us
  Pallas kernels  41.7 us (31%)
  waiting for transfers between devices  41.4 us (31%)
  starting transfers between devices  21.6 us (16%)
  blocking collectives  19.2 us (14%)
  local copies, waits for them, and re-layouts  7.99 us (6%)
  between operations  1.67 us (1%)
    all_to_all x3, waiting for transfers between devices, exchange(): return lax.all_to_all(x, AXES, split_axis=0, concat_axis=0, tiled=True)  41.4 us
    all_to_all x3, starting transfers between devices, exchange(): return lax.all_to_all(x, AXES, split_axis=0, concat_axis=0, tiled=True)  21.6 us
    all_to_all x1, blocking collectives, exchange(): return lax.all_to_all(x, AXES, split_axis=0, concat_axis=0, tiled=True)  19.2 us
    pallas_call x1, Pallas kernels, body(): call(first_kernel, (shape(blocks, 1024), shape(devices, 8, 1024)), [ANY,...  17.2 us
    pallas_call x1, Pallas kernels, body(): call(second_kernel, (shape(blocks, 1024), shape(8, blocks, dtype=F32)), [...  16.3 us
    unnamed x25, local copies, waits for them, and re-layouts  7.35 us
  transfers between devices with their start and end apart: 3, of which 3 were waited for; matrix products, arithmetic and copies ran while one was open for 0% of the time, Pallas kernels for 4%

profile of v4, /device:TPU:1, one launch (start us, length us, event | category | flops | bytes accessed | tf_op | source)
XLA Modules:
  0.0 133.6 jit_solution(1591661217539607427)
XLA Ops:
  1.3 0.8 copy.12
  2.1 0.6 concatenate.3
  2.7 11.5 %all-to-all-start = ((s32[128,1,16]{2,1,0:T(1,128)}), s32[128,1,16]{2,1,0:T(1,128)S(1)}, u32[]{:S(2)}, u32[]{:S(2)}) async-start(s32[128,1,16]{2,1,0:T(1,128)} %bitcast.2), calls=%async_computation | async-start | bytes 131072 | tf_op jit(solution)/shard_map/all_to_all | solution.py:344
  14.2 0.0 copy-start
  14.2 2.2 %copy-done = bf16[8192,256]{1,0:T(8,128)(2,1)S(1)} copy-done((bf16[8192,256]{1,0:T(8,128)(2,1)S(1)}, bf16[8192,256]{1,0:T(8,128)(2,1)}, u32[]{:S(2)}) %copy-start) | copy-done | bytes 4194328
  16.4 0.7 copy-done.10
  17.1 2.4 %shard_map.104.home_ref = bf16[128,8,256]{2,1,0:T(8,128)(2,1)S(1)} custom-call(s32[1,1024]{1,0:T(1,128)S(1)} %copy-done.10, bf16[8192,256]{1,0:T(8,128)(2,1)S(1)} %copy-done), custom_call_target="tpu_custom_call" | custom-call | flops 1073741824 | bytes 4194304 | tf_op jit(solution)/shard_map/pallas_call | solution.py:361
  19.5 0.0 copy-start.11
  19.5 0.0 copy-start.6
  19.5 4.1 %all-to-all-done = s32[128,1,16]{2,1,0:T(1,128)S(1)} async-done(((s32[128,1,16]{2,1,0:T(1,128)}), s32[128,1,16]{2,1,0:T(1,128)S(1)}, u32[]{:S(2)}, u32[]{:S(2)}) %all-to-all-start) | async-done | bytes 8224 | tf_op jit(solution)/shard_map/all_to_all | solution.py:344
  23.6 0.6 shard_map.105
  24.2 19.2 %all_to_all.20 = bf16[128,8,256]{2,1,0:T(8,128)(2,1)S(1)} all-to-all(bf16[128,8,256]{2,1,0:T(8,128)(2,1)S(1)} %shard_map.105), channel_id=1, replica_groups=mesh['slab'=4,'tile'=32] {'slab','tile'}, dimensions={0} | all-to-all | bytes 1048576 | tf_op jit(solution)/shard_map/all_to_all | solution.py:344
  43.5 2.2 %shard_map.106 = (bf16[512,256]{1,0:T(8,128)(2,1)S(1)}, bf16[128,8,256]{2,1,0:T(8,128)(2,1)}) custom-call(s32[128,16]{1,0:T(8,128)S(1)} %bitcast.12, bf16[1024,256]{1,0:T(8,128)(2,1)S(1)} %bitcast.10), custom_call_target="tpu_custom_call" | custom-call | bytes 4194304 | tf_op jit(solution)/shard_map/pallas_call | solution.py:379
  45.7 4.5 %all-to-all-start.2 = ((bf16[128,8,256]{2,1,0:T(8,128)(2,1)}), bf16[128,8,256]{2,1,0:T(8,128)(2,1)S(1)}, u32[]{:S(2)}, u32[]{:S(2)}) async-start(bf16[128,8,256]{2,1,0:T(8,128)(2,1)} %get-tuple-element.10), calls=%async_computation.2 | async-start | bytes 1048576 | tf_op jit(solution)/shard_map/all_to_all | solution.py:344
  50.3 1.7 %shard_map.107 = (bf16[512,1024]{1,0:T(8,128)(2,1)S(1)}, f32[8,512,128]{2,1,0:T(8,128)S(1)}) custom-call(bf16[512,256]{1,0:T(8,128)(2,1)S(1)} %get-tuple-element.8.parent_ref, bf16[256,1024]{1,0:T(8,128)(2,1)S(1)} %copy-done.8, bf16[3456,128]{1,0:T(8,128)(2,1)S(1)} %copy-done.6), custom_call_target="tpu_custom_call" | custom-call | flops 3221225472 | bytes 4194304 | tf_op jit(solution)/shard_map/pallas_call | solution.py:397
  52.0 1.3 copy-done.1
  53.3 1.0 copy-done.3
  54.3 9.6 %all-to-all-done.2 = bf16[128,8,256]{2,1,0:T(8,128)(2,1)S(1)} async-done(((bf16[128,8,256]{2,1,0:T(8,128)(2,1)}), bf16[128,8,256]{2,1,0:T(8,128)(2,1)S(1)}, u32[]{:S(2)}, u32[]{:S(2)}) %all-to-all-start.2) | async-done | bytes 524320 | tf_op jit(solution)/shard_map/all_to_all | solution.py:344
  63.9 17.2 %shard_map.108 = (bf16[512,1024]{1,0:T(8,128)(2,1)}, bf16[128,8,1024]{2,1,0:T(8,128)(2,1)}) custom-call(s32[13312]{0:T(1024)S(1)} %reshape.26.idx_ref, s32[128,16]{1,0:T(8,128)S(1)} %bitcast.13, bf16[512,1024]{1,0:T(8,128)(2,1)} %copy-done.3, bf16[1024,256]{1,0:T(8,128)(2,1)S(1)} %bitcast.9, bf16[256,1024]{1,0:T(8,128)(2,1)S(1)} %copy-done.8, ...), custom_call_target="tpu_custom_call" | custom-call | bytes 4194304 | tf_op jit(solution)/shard_map/pallas_call | solution.py:400
  81.2 5.6 %all-to-all-start.3 = ((bf16[128,8,1024]{2,1,0:T(8,128)(2,1)}), bf16[128,8,1024]{2,1,0:T(8,128)(2,1)}, u32[]{:S(2)}, u32[]{:S(2)}) async-start(bf16[128,8,1024]{2,1,0:T(8,128)(2,1)} %get-tuple-element.13), calls=%async_computation.3 | async-start | bytes 4194304 | tf_op jit(solution)/shard_map/all_to_all | solution.py:344
  86.9 1.2 shard_map.109.total_ref
  88.2 1.3 %copy-done.2 = f32[8,512,128]{2,1,0:T(8,128)} copy-done((f32[8,512,128]{2,1,0:T(8,128)}, f32[8,512,128]{2,1,0:T(8,128)S(1)}, u32[]{:S(2)}) %copy-start.2) | copy-done | bytes 2097176
  89.5 27.7 %all-to-all-done.3 = bf16[128,8,1024]{2,1,0:T(8,128)(2,1)} async-done(((bf16[128,8,1024]{2,1,0:T(8,128)(2,1)}), bf16[128,8,1024]{2,1,0:T(8,128)(2,1)}, u32[]{:S(2)}, u32[]{:S(2)}) %all-to-all-start.3) | async-done | bytes 2097184 | tf_op jit(solution)/shard_map/all_to_all | solution.py:344
  117.2 16.3 %shard_map.110 = (bf16[512,1024]{1,0:T(8,128)(2,1)}, f32[8,512]{1,0:T(8,128)}) custom-call(s32[13312]{0:T(1024)} %copy-done.9, bf16[512,1024]{1,0:T(8,128)(2,1)} %get-tuple-element.12.hidden_ref, bf16[1024,1024]{1,0:T(8,128)(2,1)} %bitcast.6.far_ref, bf16[3456,128]{1,0:T(8,128)(2,1)} %w_ref.7, f32[8,512,128]{2,1,0:T(8,128)} %copy-done.2, bf16[1,128]{1,0:T(2,128)(2,1)} %bitcast.15), custom_call_target="tpu_custom_call" | custom-call | bytes 4194304 | tf_op jit(solution)/shard_map/pallas_call | solution.py:417
  (18 shorter events, 0.1 us)
Async XLA Ops:
  2.7 20.9 %all-to-all-start = ((s32[128,1,16]{2,1,0:T(1,128)}), s32[128,1,16]{2,1,0:T(1,128)S(1)}, u32[]{:S(2)}, u32[]{:S(2)}) async-start(s32[128,1,16]{2,1,0:T(1,128)} %bitcast.2), calls=%async_computation | async-start | bytes 131072 | tf_op jit(solution)/shard_map/all_to_all | solution.py:344
  14.2 2.2 %copy-start = (bf16[8192,256]{1,0:T(8,128)(2,1)S(1)}, bf16[8192,256]{1,0:T(8,128)(2,1)}, u32[]{:S(2)}) copy-start(bf16[8192,256]{1,0:T(8,128)(2,1)} %coarse_ref.1) | copy-start | bytes 12582916
  16.4 0.7 copy-start.10
  19.5 30.7 %copy-start.11 = (s32[26,512]{1,0:T(8,128)S(1)}, s32[26,512]{1,0:T(8,128)}, u32[]{:S(2)}) copy-start(s32[26,512]{1,0:T(8,128)} %param.13) | copy-start | bytes 159748
  19.5 30.7 %copy-start.6 = (bf16[3456,128]{1,0:T(8,128)(2,1)S(1)}, bf16[3456,128]{1,0:T(8,128)(2,1)}, u32[]{:S(2)}) copy-start(bf16[3456,128]{1,0:T(8,128)(2,1)} %w_ref.5) | copy-start | bytes 2654212
  19.5 30.7 %copy-start.8 = (bf16[256,1024]{1,0:T(8,128)(2,1)S(1)}, bf16[256,1024]{1,0:T(8,128)(2,1)}, u32[]{:S(2)}) copy-start(bf16[256,1024]{1,0:T(8,128)(2,1)} %up_ref.3) | copy-start | bytes 1572868
  45.7 18.2 %all-to-all-start.2 = ((bf16[128,8,256]{2,1,0:T(8,128)(2,1)}), bf16[128,8,256]{2,1,0:T(8,128)(2,1)S(1)}, u32[]{:S(2)}, u32[]{:S(2)}) async-start(bf16[128,8,256]{2,1,0:T(8,128)(2,1)} %get-tuple-element.10), calls=%async_computation.2 | async-start | bytes 1048576 | tf_op jit(solution)/shard_map/all_to_all | solution.py:344
  50.2 13.7 %copy-start.9 = (s32[13312]{0:T(1024)}, s32[13312]{0:T(1024)S(1)}, u32[]{:S(2)}) copy-start(s32[13312]{0:T(1024)S(1)} %reshape.26.idx_ref) | copy-start | bytes 159748
  52.0 1.3 %copy-start.1 = (f32[8,512,128]{2,1,0:T(8,128)}, f32[8,512,128]{2,1,0:T(8,128)S(1)}, u32[]{:S(2)}) copy-start(f32[8,512,128]{2,1,0:T(8,128)S(1)} %get-tuple-element.11.total_ref) | copy-start | bytes 6291460
  53.3 1.0 copy-start.3
  81.2 5.7 %copy-start.4 = (bf16[512,1024]{1,0:T(8,128)(2,1)S(1)}, bf16[512,1024]{1,0:T(8,128)(2,1)}, u32[]{:S(2)}) copy-start(bf16[512,1024]{1,0:T(8,128)(2,1)} %copy-done.3) | copy-start | bytes 3145732
  81.2 5.7 %copy-start.5 = (bf16[512,1024]{1,0:T(8,128)(2,1)S(1)}, bf16[512,1024]{1,0:T(8,128)(2,1)}, u32[]{:S(2)}) copy-start(bf16[512,1024]{1,0:T(8,128)(2,1)} %get-tuple-element.12.hidden_ref) | copy-start | bytes 3145732
  81.2 5.7 %copy-start.7 = (bf16[3456,128]{1,0:T(8,128)(2,1)S(1)}, bf16[3456,128]{1,0:T(8,128)(2,1)}, u32[]{:S(2)}) copy-start(bf16[3456,128]{1,0:T(8,128)(2,1)} %w_ref.7) | copy-start | bytes 2654212
  81.2 36.0 %all-to-all-start.3 = ((bf16[128,8,1024]{2,1,0:T(8,128)(2,1)}), bf16[128,8,1024]{2,1,0:T(8,128)(2,1)}, u32[]{:S(2)}, u32[]{:S(2)}) async-start(bf16[128,8,1024]{2,1,0:T(8,128)(2,1)} %get-tuple-element.13), calls=%async_computation.3 | async-start | bytes 4194304 | tf_op jit(solution)/shard_map/all_to_all | solution.py:344
  88.1 1.4 %copy-start.2 = (f32[8,512,128]{2,1,0:T(8,128)}, f32[8,512,128]{2,1,0:T(8,128)S(1)}, u32[]{:S(2)}) copy-start(f32[8,512,128]{2,1,0:T(8,128)S(1)} %shard_map.109.total_ref) | copy-start | bytes 6291460
